TPU v7x, 128 devices: a whole 4x4x4 slice. The times are simulated.
128 devices in a mesh: req: 4 (over y), ctx: 32 (over z, x, core).
Axes of the slice: x: 4, y: 4, z: 4, core: 2. Of those that a mesh axis runs over, the one named last changes fastest.
Arguments:
- queries: bfloat16 [16384, 8192], P(('req', 'ctx')), parts along dimension 0, may hold values from -10 to 10
- keys: bfloat16 [131072, 1024], P(('req', 'ctx')), parts along dimension 0, may hold values from -5 to 5
- values: bfloat16 [131072, 1024], P(('req', 'ctx')), parts along dimension 0, may hold values from -6 to 6
- lengths: int32 [128], P(('req', 'ctx')), parts along dimension 0, may hold values from 128 to 1024, as said below
- owner: int32 [4], P('req'), parts along dimension 0, may hold values from 0 to 31
Outputs:
- attended: bfloat16 [512, 8192], P('req', 'ctx'), parts along dimension 0
There are 4 independent parts, one for each index of `req`. A program takes and returns all parts, laid end to end along the dimension named above; each array names one. Nothing has to cross between parts.
Inputs may be any that keep to these rules, and one draw needn't show every extreme that they name: `lengths`: multiples of 128; some block holds 1024 valid positions.
All inputs are finite; a program needn't handle non-finite values.
Results may differ from a plain program's by a relative error of at most 0.0028.
Values may be sent and summed in bfloat16 or wider, within the bound.
A program may use at most 320 MiB of HBM per device.

v0:
```python
import jax
import jax.numpy as jnp
from jax import lax
from jax.sharding import PartitionSpec as P

H = 64
KVH = 8
DH = 128


def from_root(x, axis, root):
    mine = lax.axis_index(axis) == root
    return lax.psum(jnp.where(mine, x, jnp.zeros_like(x)), axis)


def block_partial(query_rows, keys, values, valid_count):
    row_count = query_rows.shape[0]
    key_count = keys.shape[0]
    group_size = H // KVH
    valid_keys = jnp.arange(key_count, dtype=jnp.int32) < valid_count
    pieces = []
    log_parts = []
    for kv_head in range(KVH):
        query_group = query_rows[
            :, kv_head * group_size * DH : (kv_head + 1) * group_size * DH
        ].reshape(row_count, group_size, DH)
        key_head = keys[:, kv_head * DH : (kv_head + 1) * DH]
        value_head = values[:, kv_head * DH : (kv_head + 1) * DH]
        scores = jnp.einsum(
            "qgd,td->gqt", query_group, key_head, preferred_element_type=jnp.float32
        ) * DH ** (-0.5)
        scores = jnp.where(valid_keys, scores, -jnp.inf)
        highest = jnp.max(scores, axis=-1)
        weights = jnp.exp(scores - highest[..., None])
        totals = jnp.sum(weights, axis=-1)
        rounded = weights.astype(jnp.bfloat16)
        partial_value = jnp.einsum(
            "gqt,td->qgd", rounded, value_head, preferred_element_type=jnp.float32
        )
        partial_value = partial_value / jnp.transpose(totals)[:, :, None]
        pieces.append(partial_value.reshape(row_count, group_size * DH))
        log_parts.append(jnp.transpose(highest + jnp.log(totals)))
    return (jnp.concatenate(pieces, axis=1), jnp.concatenate(log_parts, axis=1))


def on_device(queries, keys, values, lengths, owner):
    devices_ctx = lax.axis_size("ctx")
    query_rows = from_root(queries, "ctx", owner[0])
    partial_value, log_total = block_partial(query_rows, keys, values, lengths[0])
    row_count = partial_value.shape[0]
    head_share = H // devices_ctx
    column_count = head_share * DH
    my_index = lax.axis_index("ctx")
    log_start = my_index * head_share
    out_start = my_index * column_count
    start_log = jnp.full((row_count, head_share), -jnp.inf, jnp.float32)
    start_out = jnp.zeros((row_count, column_count), jnp.float32)
    log_piece = lax.all_gather(log_total, "ctx", axis=0, tiled=True)
    out_piece = lax.all_gather(partial_value, "ctx", axis=0, tiled=True)
    own_logs = lax.dynamic_slice_in_dim(log_piece, log_start, head_share, 1).reshape(
        -1, row_count, head_share
    )
    own_outs = lax.dynamic_slice_in_dim(out_piece, out_start, column_count, 1).reshape(
        -1, row_count, head_share, DH
    )
    highest = jnp.max(own_logs, axis=0)
    overall = highest + jnp.log(
        jnp.exp(start_log - highest) + jnp.sum(jnp.exp(own_logs - highest[None]), axis=0)
    )
    factors = jnp.exp(own_logs - overall[None])
    added = jnp.sum(factors[..., None] * own_outs, axis=0).reshape(row_count, column_count)
    kept = jnp.repeat(jnp.exp(start_log - overall), DH, axis=1)
    overall, result = (overall, start_out * kept + added)
    return result.astype(jnp.bfloat16)


def solution(mesh):
    in_specs = (
        P(("req", "ctx"), None),
        P(("req", "ctx"), None),
        P(("req", "ctx"), None),
        P(("req", "ctx")),
        P("req"),
    )
    out_specs = P("req", "ctx")
    return jax.shard_map(
        on_device, mesh=mesh, in_specs=in_specs, out_specs=out_specs, check_vma=False
    )
```

profile of v0, /device:TPU:1, one launch (start us, length us, event | category | flops | bytes accessed | tf_op | source)
XLA Modules:
  0.0 617.6 jit_solution(11861603664457251431)
XLA Ops:
  6.5 0.0 all-reduce.2.cloned.1.call-start
  7.2 3.2 copy.35
  10.4 1.4 broadcast_select_fusion
  11.9 0.0 all-reduce.2.cloned.1.call-update
  11.9 0.0 all-gather.3.cloned.1.call-start
  12.7 110.0 %all-reduce.2.cloned.1.call-done = bf16[128,8192]{0,1:T(8,128)(2,1)} async-done(((bf16[128,8192]{0,1:T(8,128)(2,1)}), bf16[128,8192]{0,1:T(8,128)(2,1)}) %all-reduce.2.cloned.1.call-update) | async-done | bytes 2097168 | tf_op jit(solution)/shard_map/psum | solution.py:13
  122.7 1.6 fusion.155
  124.4 0.7 fusion.106
  125.1 0.0 copy-start
  125.1 0.7 fusion.108
  125.9 0.7 fusion.110
  126.6 3.0 fusion.112
  129.6 2.7 fusion.114
  132.3 0.7 fusion.118
  133.0 3.1 bitcast_reduce_fusion
  136.1 8.9 %fusion.23 = (f32[8,128]{1,0:T(8,128)S(1)}, f32[8,128]{1,0:T(8,128)S(1)}, f32[8,128]{1,0:T(8,128)S(1)}, f32[8,128]{1,0:T(8,128)S(1)}, f32[8,128]{1,0:T(8,128)S(1...) fusion(f32[128,8,1024]{2,0,1:T(8,128)} %get-tuple-element.31, ...), kind=kOutput, calls=%fused_computation.49 | convolution fusion | flops 295690240 | bytes 34120704 | tf_op jit(solution)/shard_map/qgd,td->gqt/dot_general | solution.py:29
  145.0 2.2 fusion.93
  147.1 0.0 copy-done
  147.2 0.1 copy-done.4
  147.2 7.7 %fusion.21 = (f32[8,128]{1,0:T(8,128)S(1)}, f32[8,128]{1,0:T(8,128)S(1)}, f32[8,128]{1,0:T(8,128)S(1)}, f32[8,128]{1,0:T(8,128)S(1)}, f32[8,128]{1,0:T(8,128)S(1)}, /*index=5*/f32[8,128]{1,0:T(8,128)S(1)}) fusion(f32[128,8,1024]{2,0,1:T(8,128)S(1)} %fusion.106, f32[8,128]{1,0:T(8,128)S(1)} %get-tuple-element.11, pred[1024]{0:T(1024)(128)(4,1)S(1)} %iota_compare_fusion, ...), kind=kLoop, calls=%fused_computation.47 | loop fusion | flops 25159680 | bytes 25216000 | tf_op jit(solution)/shard_map/reduce_sum | solution.py:35
  154.9 1.1 fusion.90
  156.1 1.0 copy-done.5
  157.1 1.1 fusion.87
  158.2 1.1 fusion.84
  159.3 1.1 fusion.81
  160.4 0.0 copy-start.9
  160.4 0.6 copy-done.9
  161.0 0.0 all-gather.3.cloned.1.call-update
  161.0 0.3 all-gather.5.cloned.1.call-start
  161.3 0.8 constant_dynamic-update-slice_fusion.15
  162.2 0.8 constant_dynamic-update-slice_fusion.14
  163.0 0.9 constant_dynamic-update-slice_fusion.13
  163.8 0.8 constant_dynamic-update-slice_fusion.12
  164.7 0.8 constant_dynamic-update-slice_fusion.11
  165.5 2.2 fusion.78
  167.7 0.9 constant_dynamic-update-slice_fusion.10
  168.6 2.2 fusion.75
  170.7 0.8 constant_dynamic-update-slice_fusion.9
  171.6 2.0 fusion.72
  173.6 0.8 constant_dynamic-update-slice_fusion.8
  174.4 0.0 all-gather.5.cloned.1.call-update
  174.5 29.9 %all-gather.3.cloned.1.call-done = f32[4096,64]{0,1:T(8,128)} async-done(((f32[128,64]{0,1:T(8,128)}), f32[4096,64]{0,1:T(8,128)}) %all-gather.3.cloned.1.call-update) | async-done | bytes 1048592 | tf_op jit(solution)/shard_map/all_gather | solution.py:58
  204.3 0.9 dynamic-slice_bitcast_fusion.1
  205.3 400.8 %all-gather.5.cloned.1.call-done = f32[4096,8192]{0,1:T(8,128)} async-done(((f32[128,8192]{0,1:T(8,128)}), f32[4096,8192]{0,1:T(8,128)}) %all-gather.5.cloned.1.call-update) | async-done | bytes 134217744 | tf_op jit(solution)/shard_map/all_gather | solution.py:59
  606.2 2.5 dynamic-slice_bitcast_fusion
  608.6 0.8 copy.70
  609.4 0.9 multiply_reduce_fusion
  610.3 0.7 copy.52
  (30 shorter events, 0.2 us)
Async XLA Ops:
  6.5 116.2 %all-reduce.2.cloned.1.call-start = ((), (), s32[]{:S(2)}) async-start(), calls=%async_computation | async-start | bytes 4194304 | tf_op jit(solution)/shard_map/psum | solution.py:13
  11.9 112.5 %copy-start.8 = (bf16[1024,1024]{1,0:T(8,128)(2,1)S(1)}, bf16[1024,1024]{1,0:T(8,128)(2,1)}, u32[]{:S(2)}) copy-start(bf16[1024,1024]{1,0:T(8,128)(2,1)} %param.6) | copy-start | bytes 6291460
  11.9 192.4 %all-gather.3.cloned.1.call-start = ((), (), s32[]{:S(2)}) async-start(), calls=%async_computation.1 | async-start | bytes 1081344 | tf_op jit(solution)/shard_map/all_gather | solution.py:58
  125.1 22.0 %copy-start = (f32[128,8,1024]{2,0,1:T(8,128)}, f32[128,8,1024]{2,0,1:T(8,128)S(1)}, u32[]{:S(2)}) copy-start(f32[128,8,1024]{2,0,1:T(8,128)S(1)} %fusion.106) | copy-start | bytes 12582916
  125.9 21.3 %copy-start.2 = (f32[128,8,1024]{2,0,1:T(8,128)}, f32[128,8,1024]{2,0,1:T(8,128)S(1)}, u32[]{:S(2)}) copy-start(f32[128,8,1024]{2,0,1:T(8,128)S(1)} %fusion.108) | copy-start | bytes 12582916
  145.0 2.3 copy-start.4
  147.2 7.7 %copy-start.7 = (f32[128,8,1024]{2,0,1:T(8,128)S(1)}, f32[128,8,1024]{2,0,1:T(8,128)}, u32[]{:S(2)}) copy-start(f32[128,8,1024]{2,0,1:T(8,128)} %get-tuple-element.32) | copy-start | bytes 12582916
  147.2 7.7 %copy-start.10 = (bf16[1024,1024]{1,0:T(8,128)(2,1)S(1)}, bf16[1024,1024]{1,0:T(8,128)(2,1)}, u32[]{:S(2)}) copy-start(bf16[1024,1024]{1,0:T(8,128)(2,1)} %param.7) | copy-start | bytes 6291460
  154.9 2.2 copy-start.5
  160.4 0.6 copy-start.9
  161.0 445.1 %all-gather.5.cloned.1.call-start = ((), (), s32[]{:S(2)}) async-start(), calls=%async_computation.2 | async-start | bytes 138412032 | tf_op jit(solution)/shard_map/all_gather | solution.py:59
  161.3 4.2 copy-start.3
  165.5 3.0 copy-start.1
  168.6 3.0 copy-start.6
Sparse Core Ops, SparseCore 0:
  12.0 110.6 all-reduce.1
  161.2 43.1 all-gather.2
  206.5 399.6 all-gather.4
where the time goes:
time: 618 us
  waiting for transfers between devices  541 us (88%)
  matrix products  33.4 us (5%)
  local copies, waits for them, and re-layouts  18.2 us (3%)
  between operations  14.8 us (2%)
  other arithmetic  10.1 us (2%)
    all_gather x1, waiting for transfers between devices, on_device(): out_piece = lax.all_gather(partial_value, 'ctx', axis=0, tiled=True)  401 us
    psum x1, waiting for transfers between devices, from_root(): return lax.psum(jnp.where(mine, x, jnp.zeros_like(x)), axis)  110 us
    all_gather x1, waiting for transfers between devices, on_device(): log_piece = lax.all_gather(log_total, 'ctx', axis=0, tiled=True)  29.9 us
    dot_general x8, matrix products, block_partial(): jnp.einsum('qgd,td->gqt', query_group, key_head, preferred_element_type=j...  20.5 us
    unnamed x33, local copies, waits for them, and re-layouts  15 us
    dot_general x8, matrix products, block_partial(): jnp.einsum('gqt,td->qgd', rounded, value_head, preferred_element_type=jnp...  12.8 us
  transfers between devices with their start and end apart: 3, of which 3 were waited for; matrix products, arithmetic and copies ran while one was open for 2% of the time, Pallas kernels for 0%

commit v1 on v0

v1 whole, which is shorter than its diff:
```python
import functools
import math

import jax
import jax.numpy as jnp
from jax import lax
from jax.experimental import pallas as pl
from jax.experimental.pallas import tpu as pltpu
from jax.sharding import PartitionSpec as P

H = 64
KVH = 8
DH = 128
Q = 128
BLK = 1024
GROUP = H // KVH
HALF = H * DH // 2
KV_HALF = KVH // 2
SIDE = 4
QUARTER = HALF // 2 // SIDE
ROWS = 32
CHUNKS = Q // ROWS
SCALE = DH**-0.5 * math.log2(math.e)
MESH = pl.DeviceIdType.MESH
HOPS = (2, 1, 3)
AB = (((1,), (0,)), ((), ()))


def pick(index, parts):
    out = parts[-1]
    for i in range(len(parts) - 2, -1, -1):
        out = jnp.where(index == i, parts[i], out)
    return out


def kernel(
    lengths_ref, owner_ref, queries_ref, keys_ref, values_ref, out_ref,
    cand, s1, r1, r2, qf, kraw, vraw, lens, kt, va, c1, c1l, g1, g1l, c2, g2,
    core_send, core_recv, kv_send, kv_recv, own_sem,
    q_send, q_recv, c1_send, c1_recv, c2_send, c2_recv,
):
    req = lax.axis_index("req")
    me = lax.axis_index("ctx")
    c = lax.rem(me, 2)
    x = lax.rem(me // 2, SIDE)
    z = me // (2 * SIDE)
    owner = owner_ref[0]
    owner_c = lax.rem(owner, 2)
    owner_x = lax.rem(owner // 2, SIDE)
    owner_z = owner // (2 * SIDE)

    def device(zz, xx, cc):
        return (req, (zz * SIDE + xx) * 2 + cc)

    def along_x(k):
        return lax.rem(x + k, SIDE)

    def along_z(k):
        return lax.rem(z + k, SIDE)

    sibling = device(z, x, 1 - c)

    def remote(src, dst, send, recv, to):
        return pltpu.make_async_remote_copy(
            src_ref=src, dst_ref=dst, send_sem=send, recv_sem=recv, device_id=to, device_id_type=MESH
        )

    barrier = pltpu.get_barrier_semaphore()
    peers = [sibling]
    for k in (1, 2, 3):
        peers += [device(z, along_x(k), c), device(along_z(k), x, 0), device(along_z(k), x, 1)]
    for to in peers:
        pl.semaphore_signal(barrier, inc=1, device_id=to, device_id_type=MESH)

    own_cols = pl.ds(pl.multiple_of(c * HALF, HALF), HALF)
    sib_cols = pl.ds(pl.multiple_of((1 - c) * HALF, HALF), HALF)
    kv_width = KV_HALF * DH
    own_kv = pl.ds(pl.multiple_of(c * kv_width, kv_width), kv_width)
    sib_kv = pl.ds(pl.multiple_of((1 - c) * kv_width, kv_width), kv_width)

    own = [
        pltpu.make_async_copy(
            queries_ref.at[pl.ds(ch * ROWS, ROWS), own_cols], cand.at[ch, c], own_sem.at[ch]
        )
        for ch in range(CHUNKS)
    ]
    own_k = pltpu.make_async_copy(keys_ref.at[:, own_kv], kraw.at[c], own_sem.at[CHUNKS])
    own_v = pltpu.make_async_copy(values_ref.at[:, own_kv], vraw.at[c], own_sem.at[CHUNKS + 1])
    for copy in own + [own_k, own_v]:
        copy.start()
    lens[c] = jnp.full((8, 128), lengths_ref[0], jnp.int32)

    pl.semaphore_wait(barrier, len(peers))

    core_q = [
        remote(
            queries_ref.at[pl.ds(ch * ROWS, ROWS), sib_cols], cand.at[ch, c],
            core_send.at[ch], core_recv.at[ch], sibling,
        )
        for ch in range(CHUNKS)
    ]
    core_kv = [
        remote(lens.at[c], lens.at[c], kv_send.at[0], kv_recv.at[0], sibling),
        remote(keys_ref.at[:, sib_kv], kraw.at[c], kv_send.at[1], kv_recv.at[1], sibling),
        remote(values_ref.at[:, sib_kv], vraw.at[c], kv_send.at[2], kv_recv.at[2], sibling),
    ]
    for copy in core_q + core_kv:
        copy.start()

    def quarter(index, half):
        return pl.ds(pl.multiple_of(half * (HALF // 2) + index * QUARTER, QUARTER), QUARTER)

    def spread_copies(ch, stage):
        copies = []
        for i, k in enumerate(HOPS):
            for half in range(2):
                on_x = (stage + half) % 2 == 0
                to = device(z, along_x(k), c) if on_x else device(along_z(k), x, c)
                peer = along_x(k) if on_x else along_z(k)
                here = x if on_x else z
                if stage == 0:
                    src, dst = s1.at[ch, :, quarter(peer, half)], r1.at[ch, half, here]
                elif stage == 1:
                    src = dst = r2.at[ch, half, here]
                else:
                    src = dst = qf.at[ch, :, quarter(here, half)]
                copies.append(
                    remote(src, dst, q_send.at[ch, stage, half, i], q_recv.at[ch, stage, half, i], to)
                )
        return copies

    for ch in range(CHUNKS):
        own[ch].wait()
        core_q[ch].wait_recv()
        s1[ch] = pick(owner_c, [cand[ch, 0], cand[ch, 1]])
        for copy in spread_copies(ch, 0):
            copy.start()
        r1[ch, 0, x] = s1[ch, :, quarter(x, 0)]
        r1[ch, 1, z] = s1[ch, :, quarter(z, 1)]

    def prepare(block):
        valid = lax.broadcasted_iota(jnp.int32, (BLK, DH), 0) < lens[block, 0:1, :]
        ones = jnp.where(valid, 1.0, 0.0).astype(jnp.bfloat16)
        rows = pl.ds(block * BLK, BLK)
        for kv in range(KV_HALF):
            cols = slice(kv * DH, (kv + 1) * DH)
            head = kraw[block, :, cols].astype(jnp.float32)
            head = jnp.where(valid, head, jnp.concatenate([head[:DH]] * (BLK // DH), axis=0)) * SCALE
            high = head.astype(jnp.bfloat16)
            low = (head - high.astype(jnp.float32)).astype(jnp.bfloat16)
            kt[kv, 0:DH, rows] = high.T
            kt[kv, DH : 2 * DH, rows] = low.T
            value = vraw[block, :, cols].astype(jnp.float32)
            va[kv, rows, 0:DH] = jnp.where(valid, value, 0.0).astype(jnp.bfloat16)
            va[kv, rows, DH : 2 * DH] = ones

    own_k.wait()
    own_v.wait()
    for copy in core_kv:
        copy.wait_recv()
    prepare(0)

    for ch in range(CHUNKS):
        for copy in spread_copies(ch, 0):
            copy.wait_recv()
        r2[ch, 0, z] = pick(owner_x, [r1[ch, 0, i] for i in range(SIDE)])
        r2[ch, 1, x] = pick(owner_z, [r1[ch, 1, i] for i in range(SIDE)])
        for copy in spread_copies(ch, 1):
            copy.start()

    prepare(1)

    for ch in range(CHUNKS):
        for copy in spread_copies(ch, 1):
            copy.wait_recv()
        qf[ch, :, quarter(x, 0)] = pick(owner_z, [r2[ch, 0, i] for i in range(SIDE)])
        qf[ch, :, quarter(z, 1)] = pick(owner_x, [r2[ch, 1, i] for i in range(SIDE)])
        for copy in spread_copies(ch, 2):
            copy.start()

    lane = lax.broadcasted_iota(jnp.int32, (ROWS, 128), 1)

    def scores(ch, kv):
        rows = [qf[ch, :, (kv * GROUP + i) * DH : (kv * GROUP + i + 1) * DH] for i in range(GROUP)]
        rows = jnp.concatenate(rows, axis=0)
        rows = jnp.concatenate([rows, rows], axis=1)
        return lax.dot_general(rows, kt[kv], AB, preferred_element_type=jnp.float32)

    def attend(ch, kv, s, logs):
        tops, sums = [], []
        for block in range(2):
            part = s[:, block * BLK : (block + 1) * BLK]
            top = jnp.max(part, axis=1, keepdims=True)
            weights = jnp.exp2(part - top).astype(jnp.bfloat16)
            rows = slice(block * BLK, (block + 1) * BLK)
            sums.append(lax.dot_general(weights, va[kv, rows], AB, preferred_element_type=jnp.float32))
            tops.append(top)
        highest = jnp.maximum(tops[0], tops[1])
        both = jnp.exp2(tops[0] - highest) * sums[0] + jnp.exp2(tops[1] - highest) * sums[1]
        totals = both[:, DH:]
        partial = (both[:, :DH] / totals).astype(jnp.bfloat16)
        log_total = highest + jnp.log2(totals)
        for i in range(GROUP):
            to = (kv % 2) * 2 + i // 4
            place = (kv // 2) * 4 + i % 4
            part = slice(i * ROWS, (i + 1) * ROWS)
            c1[ch, to, :, place * DH : (place + 1) * DH] = partial[part]
            logs[to] = jnp.where(lane == place, log_total[part], logs[to])

    def merge_copies(ch):
        copies = []
        for i, k in enumerate(HOPS):
            peer = along_x(k)
            to = device(z, peer, c)
            copies.append(
                remote(c1.at[ch, peer], g1.at[ch, x], c1_send.at[ch, 0, i], c1_recv.at[ch, 0, i], to)
            )
            copies.append(
                remote(c1l.at[ch, peer], g1l.at[ch, x], c1_send.at[ch, 1, i], c1_recv.at[ch, 1, i], to)
            )
        return copies

    def compute(ch):
        logs = [jnp.zeros((ROWS, 128), jnp.float32) for _ in range(SIDE)]
        s = scores(ch, 0)
        for kv in range(KV_HALF):
            later = scores(ch, kv + 1) if kv + 1 < KV_HALF else None
            attend(ch, kv, s, logs)
            s = later
        for to in range(SIDE):
            c1l[ch, to] = logs[to]
        for copy in merge_copies(ch):
            copy.start()
        g1[ch, x] = c1[ch, x]
        g1l[ch, x] = c1l[ch, x]

    def weigh(parts):
        top = functools.reduce(jnp.maximum, parts)
        factors = [jnp.exp2(part - top) for part in parts]
        total = functools.reduce(jnp.add, factors)
        return [factor / total for factor in factors], top + jnp.log2(total)

    def finals(ch, act):
        for zi in range(2):
            for core in range(2):
                place = zi * 2 + core
                zz = 2 * c + zi
                here = jnp.logical_and(zz == z, core == c)
                copy = remote(
                    c2.at[ch, place], g2.at[ch, z], c2_send.at[ch, place], c2_recv.at[ch, z], device(zz, x, core)
                )
                act(place, here, copy)

    def merge(ch):
        for copy in merge_copies(ch):
            copy.wait_recv()
        factors, logs = weigh([g1l[ch, i] for i in range(SIDE)])
        for head in range(8):
            cols = slice(head * DH, (head + 1) * DH)
            added = functools.reduce(
                jnp.add,
                [factors[i][:, head : head + 1] * g1[ch, i, :, cols].astype(jnp.float32) for i in range(SIDE)],
            )
            c2[ch, head // 2, :, (head % 2) * DH : (head % 2 + 1) * DH] = added
        for place in range(4):
            c2[ch, place, :, 2 * DH :] = logs

        def send(place, here, copy):
            @pl.when(jnp.logical_not(here))
            def _():
                copy.start()

            @pl.when(here)
            def _():
                g2[ch, z] = c2[ch, place]

        finals(ch, send)

    def finish(ch):
        for zz in range(SIDE):
            @pl.when(jnp.logical_or(zz != z, z // 2 != c))
            def _():
                remote(
                    c2.at[ch, 0], g2.at[ch, zz], c2_send.at[ch, 0], c2_recv.at[ch, zz], sibling
                ).wait_recv()

        for idx in range(2):
            mine = lane == lax.rem(z, 2) * 4 + c * 2 + idx
            logs = [
                jnp.sum(jnp.where(mine, g2[ch, i, :, 2 * DH :], 0.0), axis=1, keepdims=True) for i in range(SIDE)
            ]
            factors, _ = weigh(logs)
            cols = slice(idx * DH, (idx + 1) * DH)
            added = functools.reduce(jnp.add, [factors[i] * g2[ch, i, :, cols] for i in range(SIDE)])
            out_ref[ch * ROWS : (ch + 1) * ROWS, cols] = added.astype(jnp.bfloat16)

    for ch in range(CHUNKS):
        for copy in spread_copies(ch, 2):
            copy.wait_recv()
        compute(ch)
        if ch > 0:
            merge(ch - 1)
    merge(CHUNKS - 1)
    for ch in range(CHUNKS):
        finish(ch)

    for copy in core_q + core_kv:
        copy.wait_send()
    for ch in range(CHUNKS):
        for stage in range(3):
            for copy in spread_copies(ch, stage):
                copy.wait_send()
        for copy in merge_copies(ch):
            copy.wait_send()

        def left(place, here, copy):
            @pl.when(jnp.logical_not(here))
            def _():
                copy.wait_send()

        finals(ch, left)


def on_device(queries, keys, values, lengths, owner):
    vmem, dma = pltpu.VMEM, pltpu.SemaphoreType.DMA
    any_space = pl.BlockSpec(memory_space=pl.ANY)
    smem = pl.BlockSpec(memory_space=pltpu.SMEM)
    bf16, f32 = jnp.bfloat16, jnp.float32
    return pl.pallas_call(
        kernel,
        out_shape=jax.ShapeDtypeStruct((Q, 2 * DH), bf16),
        in_specs=[smem, smem, any_space, any_space, any_space],
        out_specs=pl.BlockSpec(memory_space=vmem),
        scratch_shapes=[
            vmem((CHUNKS, 2, ROWS, HALF), bf16),
            vmem((CHUNKS, ROWS, HALF), bf16),
            vmem((CHUNKS, 2, SIDE, ROWS, QUARTER), bf16),
            vmem((CHUNKS, 2, SIDE, ROWS, QUARTER), bf16),
            vmem((CHUNKS, ROWS, HALF), bf16),
            vmem((2, BLK, KV_HALF * DH), bf16),
            vmem((2, BLK, KV_HALF * DH), bf16),
            vmem((2, 8, 128), jnp.int32),
            vmem((KV_HALF, 2 * DH, 2 * BLK), bf16),
            vmem((KV_HALF, 2 * BLK, 2 * DH), bf16),
            vmem((CHUNKS, SIDE, ROWS, 8 * DH), bf16),
            vmem((CHUNKS, SIDE, ROWS, 128), f32),
            vmem((CHUNKS, SIDE, ROWS, 8 * DH), bf16),
            vmem((CHUNKS, SIDE, ROWS, 128), f32),
            vmem((CHUNKS, 4, ROWS, 3 * DH), f32),
            vmem((CHUNKS, SIDE, ROWS, 3 * DH), f32),
            dma((CHUNKS,)), dma((CHUNKS,)),
            dma((3,)), dma((3,)),
            dma((CHUNKS + 2,)),
            dma((CHUNKS, 3, 2, 3)), dma((CHUNKS, 3, 2, 3)),
            dma((CHUNKS, 2, 3)), dma((CHUNKS, 2, 3)),
            dma((CHUNKS, 4)), dma((CHUNKS, SIDE)),
        ],
        compiler_params=pltpu.CompilerParams(
            collective_id=0, has_side_effects=True, vmem_limit_bytes=56 * 2**20
        ),
        cost_estimate=pl.CostEstimate(
            flops=4 * H * Q * BLK * DH, bytes_accessed=6 * 2**20, transcendentals=H * Q * BLK
        ),
    )(lengths, owner, queries, keys, values)


def solution(mesh):
    in_specs = (
        P(("req", "ctx"), None),
        P(("req", "ctx"), None),
        P(("req", "ctx"), None),
        P(("req", "ctx")),
        P("req"),
    )
    return jax.shard_map(
        on_device, mesh=mesh, in_specs=in_specs, out_specs=P("req", "ctx"), check_vma=False
    )
```

time: 618 us -> 56 us (0.09)
  waiting for transfers between devices: 541 us -> 0 us
  Pallas kernels: 0 us -> 53 us
  matrix products: 33.4 us -> 0 us
  local copies, waits for them, and re-layouts: 18.2 us -> 1.47 us
  between operations: 14.8 us -> 1.31 us
  other arithmetic: 10.1 us -> 0 us
    all_gather x2 -> x0, waiting for transfers between devices: 431 us -> none  [the longest x1 401 us: on_device(): out_piece = lax.all_gather(partial_value, 'ctx', axis=0, tiled=True)]
    psum x1 -> x0, waiting for transfers between devices: 110 us -> none  [from_root(): return lax.psum(jnp.where(mine, x, jnp.zeros_like(x)), axis)]
    pallas_call x0 -> x1, Pallas kernels: none -> 53 us  [on_device(): pl.pallas_call(kernel, out_shape=jax.ShapeDtypeStruct((Q, 2 * DH), bf16),...]
    dot_general x16 -> x0, matrix products: 33.4 us -> none  [the longest x8 20.5 us: block_partial(): jnp.einsum('qgd,td->gqt', query_group, key_head, preferred_element_type=j...]
    unnamed x33 -> x1, local copies, waits for them, and re-layouts: 15 us -> 1.47 us
    reduce_sum x3 -> x0, other arithmetic: 8.58 us -> none  [the longest x1 7.66 us: block_partial(): totals = jnp.sum(weights, axis=-1)]
  transfers between devices with their start and end apart: 3 -> 0, of which waited for: 3 -> 0; matrix products, arithmetic and copies ran while one was open for 2% -> 0% of each run, Pallas kernels for 0% -> 0%
where the time goes in v1:
time: 56 us; the launch traced here: 55.8 us
  Pallas kernels  53 us (95%)
  local copies, waits for them, and re-layouts  1.47 us (3%)
  between operations  1.31 us (2%)
    pallas_call x1, Pallas kernels, on_device(): pl.pallas_call(kernel, out_shape=jax.ShapeDtypeStruct((Q, 2 * DH), bf16),...  53 us
    unnamed x1, local copies, waits for them, and re-layouts  1.47 us

profile of v1, /device:TPU:1, one launch (start us, length us, event | category | flops | bytes accessed | tf_op | source)
XLA Modules:
  0.0 55.8 jit_solution(4177790219677418422)
XLA Ops:
  1.3 53.0 %shard_map.55 = bf16[128,256]{1,0:T(8,128)(2,1)} custom-call(s32[1]{0:T(128)S(6)} %copy.7.lengths_ref, s32[1]{0:T(128)S(6)} %copy.8.owner_ref, bf16[128,8192]{1,0:T(8,128)(2,1)} %queries_ref.1, bf16[1024,1024]{1,0:T(8,128)(2,1)} %keys_ref.1, bf16[1024,1024]{1,0:T(8,128)(2,1)} %values_ref.1), custom_call_target="tpu_custom_call" | custom-call | flops 4294967296 | bytes 6291456 | tf_op jit(solution)/shard_map/pallas_call | solution.py:329
  54.3 1.5 %copy.9 = bf16[128,256]{1,0:T(8,128)(2,1)} copy(bf16[128,256]{1,0:T(8,128)(2,1)} %shard_map.55) | data formatting | bytes 131072

commit v2 on v1

v2 whole, which is shorter than its diff:
```python
import functools
import math

import jax
import jax.numpy as jnp
from jax import lax
from jax.experimental import pallas as pl
from jax.experimental.pallas import tpu as pltpu
from jax.sharding import PartitionSpec as P

H = 64
KVH = 8
DH = 128
Q = 128
BLK = 1024
GROUP = H // KVH
HALF = H * DH // 2
KV_HALF = KVH // 2
SIDE = 4
QUARTER = HALF // 2 // SIDE
ROWS = 32
CHUNKS = Q // ROWS
SCALE = DH**-0.5 * math.log2(math.e)
STEPS = 32000.0
TINY = 1e-30
MESH = pl.DeviceIdType.MESH
HOPS = (2, 1, 3)
AB = (((1,), (0,)), ((), ()))


def pick(index, parts):
    out = parts[-1]
    for i in range(len(parts) - 2, -1, -1):
        out = jnp.where(index == i, parts[i], out)
    return out


def kernel(
    lengths_ref, owner_ref, queries_ref, keys_ref, values_ref, out_ref,
    cand, s1, r1, r2, qf, raw, lens, kt, va,
    ca, sa, cb, sb, ga, gsa, gb, gsb, da, db, ha, hb,
    core_send, core_recv, kv_send, kv_recv, own_sem, q_send, q_recv,
    first_send, first_recv, second_send, second_recv,
):
    req = lax.axis_index("req")
    me = lax.axis_index("ctx")
    c = lax.rem(me, 2)
    x = lax.rem(me // 2, SIDE)
    z = me // (2 * SIDE)
    owner = owner_ref[0]
    owner_c = lax.rem(owner, 2)
    owner_x = lax.rem(owner // 2, SIDE)
    owner_z = owner // (2 * SIDE)

    def device(zz, xx, cc):
        return (req, (zz * SIDE + xx) * 2 + cc)

    def along_x(k):
        return lax.rem(x + k, SIDE)

    def along_z(k):
        return lax.rem(z + k, SIDE)

    sibling = device(z, x, 1 - c)

    def wait(ref, sem):
        pltpu.make_async_copy(ref, ref, sem).wait()

    def remote(src, dst, send, recv, to):
        return pltpu.make_async_remote_copy(
            src_ref=src, dst_ref=dst, send_sem=send, recv_sem=recv, device_id=to, device_id_type=MESH
        )

    barrier = pltpu.get_barrier_semaphore()
    peers = [sibling]
    for k in (1, 2, 3):
        for core in range(2):
            peers += [device(z, along_x(k), core), device(along_z(k), x, core)]
    for to in peers:
        pl.semaphore_signal(barrier, inc=1, device_id=to, device_id_type=MESH)

    own_cols = pl.ds(pl.multiple_of(c * HALF, HALF), HALF)
    sib_cols = pl.ds(pl.multiple_of((1 - c) * HALF, HALF), HALF)
    kv_width = KV_HALF * DH
    own_kv = pl.ds(pl.multiple_of(c * kv_width, kv_width), kv_width)
    sib_kv = pl.ds(pl.multiple_of((1 - c) * kv_width, kv_width), kv_width)

    own = [
        pltpu.make_async_copy(
            queries_ref.at[pl.ds(ch * ROWS, ROWS), own_cols], cand.at[ch, c], own_sem.at[ch]
        )
        for ch in range(CHUNKS)
    ]
    own_k = pltpu.make_async_copy(keys_ref.at[:, own_kv], raw.at[c, 0], own_sem.at[CHUNKS])
    own_v = pltpu.make_async_copy(values_ref.at[:, own_kv], raw.at[c, 1], own_sem.at[CHUNKS + 1])
    for copy in own + [own_k, own_v]:
        copy.start()
    lens[c] = jnp.full((8, 128), lengths_ref[0], jnp.int32)

    pl.semaphore_wait(barrier, len(peers))

    core_q = [
        remote(
            queries_ref.at[pl.ds(ch * ROWS, ROWS), sib_cols], cand.at[ch, c],
            core_send, core_recv.at[ch], sibling,
        )
        for ch in range(CHUNKS)
    ]
    core_kv = [
        remote(lens.at[c], lens.at[c], kv_send.at[0], kv_recv.at[0], sibling),
        remote(keys_ref.at[:, sib_kv], raw.at[c, 0], kv_send.at[1], kv_recv.at[1], sibling),
        remote(values_ref.at[:, sib_kv], raw.at[c, 1], kv_send.at[1], kv_recv.at[1], sibling),
    ]
    for copy in core_q + core_kv:
        copy.start()

    def quarter(index, half):
        return pl.ds(pl.multiple_of(half * (HALF // 2) + index * QUARTER, QUARTER), QUARTER)

    def spread_copies(ch, stage):
        copies = []
        for k in HOPS:
            for half in range(2):
                on_x = (stage + half) % 2 == 0
                to = device(z, along_x(k), c) if on_x else device(along_z(k), x, c)
                peer = along_x(k) if on_x else along_z(k)
                here = x if on_x else z
                if stage == 0:
                    src, dst = s1.at[ch, :, quarter(peer, half)], r1.at[ch, half, here]
                elif stage == 1:
                    src = dst = r2.at[ch, half, here]
                else:
                    src = dst = qf.at[ch, :, quarter(here, half)]
                copies.append(remote(src, dst, q_send.at[stage], q_recv.at[ch, stage], to))
        return copies

    def spread_wait(ch, stage):
        wait(r1.at[ch, :, 0 : SIDE - 1], q_recv.at[ch, stage])

    for ch in range(CHUNKS):
        own[ch].wait()
        core_q[ch].wait_recv()
        s1[ch] = pick(owner_c, [cand[ch, 0], cand[ch, 1]])
        for copy in spread_copies(ch, 0):
            copy.start()
        r1[ch, 0, x] = s1[ch, :, quarter(x, 0)]
        r1[ch, 1, z] = s1[ch, :, quarter(z, 1)]

    def prepare(block):
        valid = lax.broadcasted_iota(jnp.int32, (BLK, DH), 0) < lens[block, 0:1, :]
        ones = jnp.where(valid, 1.0, 0.0).astype(jnp.bfloat16)
        rows = pl.ds(block * BLK, BLK)
        for kv in range(KV_HALF):
            cols = slice(kv * DH, (kv + 1) * DH)
            head = raw[block, 0, :, cols].astype(jnp.float32)
            head = jnp.where(valid, head, jnp.concatenate([head[:DH]] * (BLK // DH), axis=0)) * SCALE
            high = head.astype(jnp.bfloat16)
            low = (head - high.astype(jnp.float32)).astype(jnp.bfloat16)
            kt[kv, 0:DH, rows] = high.T
            kt[kv, DH : 2 * DH, rows] = low.T
            value = raw[block, 1, :, cols].astype(jnp.float32)
            va[kv, rows, 0:DH] = jnp.where(valid, value, 0.0).astype(jnp.bfloat16)
            va[kv, rows, DH : 2 * DH] = ones

    own_k.wait()
    own_v.wait()
    wait(lens.at[0], kv_recv.at[0])
    wait(raw.at[0], kv_recv.at[1])
    prepare(0)

    for ch in range(CHUNKS):
        spread_wait(ch, 0)
        r2[ch, 0, z] = pick(owner_x, [r1[ch, 0, i] for i in range(SIDE)])
        r2[ch, 1, x] = pick(owner_z, [r1[ch, 1, i] for i in range(SIDE)])
        for copy in spread_copies(ch, 1):
            copy.start()

    prepare(1)

    for ch in range(CHUNKS):
        spread_wait(ch, 1)
        qf[ch, :, quarter(x, 0)] = pick(owner_z, [r2[ch, 0, i] for i in range(SIDE)])
        qf[ch, :, quarter(z, 1)] = pick(owner_x, [r2[ch, 1, i] for i in range(SIDE)])
        for copy in spread_copies(ch, 2):
            copy.start()

    diagonal = lax.broadcasted_iota(jnp.int32, (ROWS, 128), 0) == lax.broadcasted_iota(jnp.int32, (ROWS, 128), 1)

    def to_row(wide):
        return jnp.sum(jnp.where(diagonal, wide, 0.0), axis=-2)

    def to_column(row):
        return jnp.sum(jnp.where(diagonal, row, 0.0), axis=1, keepdims=True)

    def scores(ch, kv):
        rows = [qf[ch, :, (kv * GROUP + i) * DH : (kv * GROUP + i + 1) * DH] for i in range(GROUP)]
        rows = jnp.concatenate(rows, axis=0)
        rows = jnp.concatenate([rows, rows], axis=1)
        return lax.dot_general(rows, kt[kv], AB, preferred_element_type=jnp.float32)

    def attend(ch, kv, s):
        tops, sums = [], []
        for block in range(2):
            part = s[:, block * BLK : (block + 1) * BLK]
            top = jnp.max(part, axis=1, keepdims=True)
            weights = jnp.exp2(part - top).astype(jnp.bfloat16)
            rows = slice(block * BLK, (block + 1) * BLK)
            sums.append(lax.dot_general(weights, va[kv, rows], AB, preferred_element_type=jnp.float32))
            tops.append(top)
        highest = jnp.maximum(tops[0], tops[1])
        both = jnp.exp2(tops[0] - highest) * sums[0] + jnp.exp2(tops[1] - highest) * sums[1]
        totals = both[:, DH:]
        largest = jnp.max(jnp.abs(both[:, :DH]), axis=1, keepdims=True)
        largest = jnp.maximum(largest, TINY)
        partial = jnp.round(both[:, :DH] * (STEPS / largest)).astype(jnp.int32).astype(jnp.int16)
        step = largest * (1.0 / STEPS) / totals
        log_total = highest + jnp.log2(totals)
        log_rows = to_row(log_total.reshape(GROUP, ROWS, DH))
        step_rows = to_row(step.reshape(GROUP, ROWS, DH))
        zi = kv // 2
        for i in range(GROUP):
            xx, core = (kv % 2) * 2 + i // 4, (i % 4) // 2
            part = partial[i * ROWS : (i + 1) * ROWS]
            if i % 2 == 0:
                place, to, box, stats, count = zi * 2 + core, xx, ca, sa, 4
            else:
                place, to, box, stats, count = xx * 2 + core, zi, cb, sb, 8
            box[ch, to, :, place * DH : (place + 1) * DH] = part
            stats[ch, to, place : place + 1] = log_rows[i : i + 1]
            stats[ch, to, count + place : count + place + 1] = step_rows[i : i + 1]

    merger = c == z // 2

    def first_copies(ch, act):
        for k in HOPS:
            peer = along_x(k)
            to = device(z, peer, c)
            act(True, remote(ca.at[ch, peer], ga.at[ch, x], first_send.at[0], first_recv.at[ch, 0], to))
            act(True, remote(sa.at[ch, peer], gsa.at[ch, x], first_send.at[1], first_recv.at[ch, 1], to))
        for zi in range(2):
            zz = 2 * c + zi
            to = device(zz, x, c)
            act(zz != z, remote(cb.at[ch, zi], gb.at[ch, z], first_send.at[2], first_recv.at[ch, 2], to))
            act(zz != z, remote(sb.at[ch, zi], gsb.at[ch, z], first_send.at[3], first_recv.at[ch, 3], to))

    def act_start(condition, copy):
        if condition is True:
            copy.start()
        else:
            @pl.when(condition)
            def _():
                copy.start()

    def compute(ch):
        s = scores(ch, 0)
        for kv in range(KV_HALF):
            later = scores(ch, kv + 1) if kv + 1 < KV_HALF else None
            attend(ch, kv, s)
            s = later
        first_copies(ch, act_start)
        ga[ch, x] = ca[ch, x]
        gsa[ch, x] = sa[ch, x]

        @pl.when(merger)
        def _():
            zi = lax.rem(z, 2)
            gb[ch, z] = cb[ch, zi]
            gsb[ch, z] = sb[ch, zi]

    def weigh(parts):
        top = functools.reduce(jnp.maximum, parts)
        factors = [jnp.exp2(part - top) for part in parts]
        total = functools.reduce(jnp.add, factors)
        return [factor / total for factor in factors], top + jnp.log2(total)

    def merge_side(ch, count, got, stats, done):
        tiles = [stats[ch, i] for i in range(SIDE)]
        factors, logs = weigh([tile[:count] for tile in tiles])
        scales = [factors[i] * tiles[i][count : 2 * count] for i in range(SIDE)]
        for head in range(count):
            cols = slice(head * DH, (head + 1) * DH)
            added = functools.reduce(
                jnp.add,
                [
                    to_column(scales[i][head : head + 1]) * got[ch, i, :, cols].astype(jnp.int32).astype(jnp.float32)
                    for i in range(SIDE)
                ],
            )
            done[ch, head, 0:ROWS] = added
            done[ch, head, ROWS : ROWS + 8] = jnp.broadcast_to(logs[head : head + 1], (8, 128))

    def merge(ch):
        wait(ga.at[ch, 0 : SIDE - 1], first_recv.at[ch, 0])
        wait(gsa.at[ch, 0 : SIDE - 1], first_recv.at[ch, 1])
        merge_side(ch, 4, ga, gsa, da)
        for place in range(4):
            zz, core = 2 * c + place // 2, place % 2
            here = jnp.logical_and(zz == z, core == c)
            act_start(
                jnp.logical_not(here),
                remote(
                    da.at[ch, place], ha.at[ch, z], second_send.at[0], second_recv.at[ch, 0], device(zz, x, core)
                ),
            )

            @pl.when(here)
            def _():
                ha[ch, z] = da[ch, place]

        @pl.when(merger)
        def _():
            wait(gb.at[ch, 0 : SIDE - 1], first_recv.at[ch, 2])
            wait(gsb.at[ch, 0 : SIDE - 1], first_recv.at[ch, 3])
            merge_side(ch, 8, gb, gsb, db)
            for place in range(8):
                xx, core = place // 2, place % 2
                here = jnp.logical_and(xx == x, core == c)
                act_start(
                    jnp.logical_not(here),
                    remote(
                        db.at[ch, place], hb.at[ch, x], second_send.at[1], second_recv.at[ch, 1], device(z, xx, core)
                    ),
                )

                @pl.when(here)
                def _():
                    hb[ch, x] = db[ch, place]

    def finish(ch):
        for side, got in ((0, ha), (1, hb)):
            @pl.when(merger)
            def _():
                wait(got.at[ch, 0 : SIDE - 1], second_recv.at[ch, side])

            @pl.when(jnp.logical_not(merger))
            def _():
                wait(got.at[ch], second_recv.at[ch, side])

            factors, _ = weigh([got[ch, i, ROWS : ROWS + 1] for i in range(SIDE)])
            added = functools.reduce(jnp.add, [to_column(factors[i]) * got[ch, i, 0:ROWS] for i in range(SIDE)])
            out_ref[ch * ROWS : (ch + 1) * ROWS, side * DH : (side + 1) * DH] = added.astype(jnp.bfloat16)

    for ch in range(CHUNKS):
        spread_wait(ch, 2)
        compute(ch)
        if ch > 0:
            merge(ch - 1)
    merge(CHUNKS - 1)
    for ch in range(CHUNKS):
        finish(ch)

    wait(cand.at[:, 0], core_send)
    wait(lens.at[0], kv_send.at[0])
    wait(raw.at[0], kv_send.at[1])
    for stage in range(3):
        wait(r1.at[:, :, 0 : SIDE - 1], q_send.at[stage])
    wait(ga.at[:, 0 : SIDE - 1], first_send.at[0])
    wait(gsa.at[:, 0 : SIDE - 1], first_send.at[1])

    @pl.when(merger)
    def _():
        wait(gb.at[:, 0:1], first_send.at[2])
        wait(gsb.at[:, 0:1], first_send.at[3])
        wait(da.at[:, 0:3], second_send.at[0])
        wait(db.at[:, 0:7], second_send.at[1])

    @pl.when(jnp.logical_not(merger))
    def _():
        wait(gb.at[:, 0:2], first_send.at[2])
        wait(gsb.at[:, 0:2], first_send.at[3])
        wait(da, second_send.at[0])


def on_device(queries, keys, values, lengths, owner):
    vmem, dma = pltpu.VMEM, pltpu.SemaphoreType.DMA
    any_space = pl.BlockSpec(memory_space=pl.ANY)
    smem = pl.BlockSpec(memory_space=pltpu.SMEM)
    bf16, f32, i16 = jnp.bfloat16, jnp.float32, jnp.int16
    return pl.pallas_call(
        kernel,
        out_shape=jax.ShapeDtypeStruct((Q, 2 * DH), bf16),
        in_specs=[smem, smem, any_space, any_space, any_space],
        out_specs=pl.BlockSpec(memory_space=vmem),
        scratch_shapes=[
            vmem((CHUNKS, 2, ROWS, HALF), bf16),
            vmem((CHUNKS, ROWS, HALF), bf16),
            vmem((CHUNKS, 2, SIDE, ROWS, QUARTER), bf16),
            vmem((CHUNKS, 2, SIDE, ROWS, QUARTER), bf16),
            vmem((CHUNKS, ROWS, HALF), bf16),
            vmem((2, 2, BLK, KV_HALF * DH), bf16),
            vmem((2, 8, 128), jnp.int32),
            vmem((KV_HALF, 2 * DH, 2 * BLK), bf16),
            vmem((KV_HALF, 2 * BLK, 2 * DH), bf16),
            vmem((CHUNKS, SIDE, ROWS, 4 * DH), i16),
            vmem((CHUNKS, SIDE, 8, 128), f32),
            vmem((CHUNKS, 2, ROWS, 8 * DH), i16),
            vmem((CHUNKS, 2, 16, 128), f32),
            vmem((CHUNKS, SIDE, ROWS, 4 * DH), i16),
            vmem((CHUNKS, SIDE, 8, 128), f32),
            vmem((CHUNKS, SIDE, ROWS, 8 * DH), i16),
            vmem((CHUNKS, SIDE, 16, 128), f32),
            vmem((CHUNKS, 4, ROWS + 8, DH), f32),
            vmem((CHUNKS, 8, ROWS + 8, DH), f32),
            vmem((CHUNKS, SIDE, ROWS + 8, DH), f32),
            vmem((CHUNKS, SIDE, ROWS + 8, DH), f32),
            dma, dma((CHUNKS,)),
            dma((2,)), dma((2,)),
            dma((CHUNKS + 2,)),
            dma((3,)), dma((CHUNKS, 3)),
            dma((4,)), dma((CHUNKS, 4)),
            dma((2,)), dma((CHUNKS, 2)),
        ],
        compiler_params=pltpu.CompilerParams(
            collective_id=0, has_side_effects=True, vmem_limit_bytes=56 * 2**20
        ),
        cost_estimate=pl.CostEstimate(
            flops=4 * H * Q * BLK * DH, bytes_accessed=6 * 2**20, transcendentals=H * Q * BLK
        ),
    )(lengths, owner, queries, keys, values)


def solution(mesh):
    in_specs = (
        P(("req", "ctx"), None),
        P(("req", "ctx"), None),
        P(("req", "ctx"), None),
        P(("req", "ctx")),
        P("req"),
    )
    return jax.shard_map(
        on_device, mesh=mesh, in_specs=in_specs, out_specs=P("req", "ctx"), check_vma=False
    )
```

time: 56 us -> 50.8 us (0.907)
  Pallas kernels: 53 us -> 47.9 us
    pallas_call x1, Pallas kernels: 53 us -> 47.9 us  [on_device(): pl.pallas_call(kernel, out_shape=jax.ShapeDtypeStruct((Q, 2 * DH), bf16),...]
where the time goes in v2:
time: 50.8 us; the launch traced here: 50.6 us
  Pallas kernels  47.9 us (94%)
  local copies, waits for them, and re-layouts  1.47 us (3%)
  between operations  1.31 us (3%)
    pallas_call x1, Pallas kernels, on_device(): pl.pallas_call(kernel, out_shape=jax.ShapeDtypeStruct((Q, 2 * DH), bf16),...  47.9 us
    unnamed x1, local copies, waits for them, and re-layouts  1.47 us

profile of v2, /device:TPU:1, one launch (start us, length us, event | category | flops | bytes accessed | tf_op | source)
XLA Modules:
  0.0 50.6 jit_solution(15419199320035859465)
XLA Ops:
  1.3 47.9 %shard_map.55 = bf16[128,256]{1,0:T(8,128)(2,1)} custom-call(s32[1]{0:T(128)S(6)} %copy.7.lengths_ref, s32[1]{0:T(128)S(6)} %copy.8.owner_ref, bf16[128,8192]{1,0:T(8,128)(2,1)} %queries_ref.1, bf16[1024,1024]{1,0:T(8,128)(2,1)} %keys_ref.1, bf16[1024,1024]{1,0:T(8,128)(2,1)} %values_ref.1), custom_call_target="tpu_custom_call" | custom-call | flops 4294967296 | bytes 6291456 | tf_op jit(solution)/shard_map/pallas_call | solution.py:379
  49.2 1.5 %copy.9 = bf16[128,256]{1,0:T(8,128)(2,1)} copy(bf16[128,256]{1,0:T(8,128)(2,1)} %shard_map.55) | data formatting | bytes 131072

commit v3 on v2

--- a/solution.py
+++ b/solution.py
@@ -18,14 +18,37 @@
 KV_HALF = KVH // 2
 SIDE = 4
 QUARTER = HALF // 2 // SIDE
-ROWS = 32
-CHUNKS = Q // ROWS
+SIZES = (32, 64, 32)
+CHUNKS = len(SIZES)
+STARTS = tuple(sum(SIZES[:ch]) for ch in range(CHUNKS))
 SCALE = DH**-0.5 * math.log2(math.e)
 STEPS = 32000.0
 TINY = 1e-30
 MESH = pl.DeviceIdType.MESH
 HOPS = (2, 1, 3)
 AB = (((1,), (0,)), ((), ()))
+
+
+ORDER = (
+    *[("offer", ch) for ch in range(CHUNKS)],
+    ("keys",),
+    ("prepare", 0),
+    *[("across", ch) for ch in range(CHUNKS)],
+    ("prepare", 1),
+    *[("gather", ch) for ch in range(CHUNKS)],
+    ("arrive", 0), ("compute", 0),
+    ("arrive", 1), ("compute", 1), ("merge", 0),
+    ("arrive", 2), ("compute", 2), ("merge", 1),
+    ("finish", 0), ("merge", 2), ("finish", 1), ("finish", 2),
+)
+
+
+def rows_of(ch):
+    return pl.ds(STARTS[ch], SIZES[ch])
+
+
+def boxed(ch):
+    return pl.ds(STARTS[ch] + 8 * ch, SIZES[ch] + 8)
 
 
 def pick(index, parts):
@@ -87,7 +110,7 @@
 
     own = [
         pltpu.make_async_copy(
-            queries_ref.at[pl.ds(ch * ROWS, ROWS), own_cols], cand.at[ch, c], own_sem.at[ch]
+            queries_ref.at[rows_of(ch), own_cols], cand.at[c, rows_of(ch)], own_sem.at[ch]
         )
         for ch in range(CHUNKS)
     ]
@@ -101,7 +124,7 @@
 
     core_q = [
         remote(
-            queries_ref.at[pl.ds(ch * ROWS, ROWS), sib_cols], cand.at[ch, c],
+            queries_ref.at[rows_of(ch), sib_cols], cand.at[c, rows_of(ch)],
             core_send, core_recv.at[ch], sibling,
         )
         for ch in range(CHUNKS)
@@ -126,25 +149,26 @@
                 peer = along_x(k) if on_x else along_z(k)
                 here = x if on_x else z
                 if stage == 0:
-                    src, dst = s1.at[ch, :, quarter(peer, half)], r1.at[ch, half, here]
+                    src, dst = s1.at[rows_of(ch), quarter(peer, half)], r1.at[half, here, rows_of(ch)]
                 elif stage == 1:
-                    src = dst = r2.at[ch, half, here]
+                    src = dst = r2.at[half, here, rows_of(ch)]
                 else:
-                    src = dst = qf.at[ch, :, quarter(here, half)]
+                    src = dst = qf.at[rows_of(ch), quarter(here, half)]
                 copies.append(remote(src, dst, q_send.at[stage], q_recv.at[ch, stage], to))
         return copies
 
     def spread_wait(ch, stage):
-        wait(r1.at[ch, :, 0 : SIDE - 1], q_recv.at[ch, stage])
-
-    for ch in range(CHUNKS):
+        wait(r1.at[:, 0 : SIDE - 1, rows_of(ch)], q_recv.at[ch, stage])
+
+    def offer(ch):
         own[ch].wait()
         core_q[ch].wait_recv()
-        s1[ch] = pick(owner_c, [cand[ch, 0], cand[ch, 1]])
+        rows = rows_of(ch)
+        s1[rows] = pick(owner_c, [cand[0, rows], cand[1, rows]])
         for copy in spread_copies(ch, 0):
             copy.start()
-        r1[ch, 0, x] = s1[ch, :, quarter(x, 0)]
-        r1[ch, 1, z] = s1[ch, :, quarter(z, 1)]
+        r1[0, x, rows] = s1[rows, quarter(x, 0)]
+        r1[1, z, rows] = s1[rows, quarter(z, 1)]
 
     def prepare(block):
         valid = lax.broadcasted_iota(jnp.int32, (BLK, DH), 0) < lens[block, 0:1, :]
@@ -162,38 +186,39 @@
             va[kv, rows, 0:DH] = jnp.where(valid, value, 0.0).astype(jnp.bfloat16)
             va[kv, rows, DH : 2 * DH] = ones
 
-    own_k.wait()
-    own_v.wait()
-    wait(lens.at[0], kv_recv.at[0])
-    wait(raw.at[0], kv_recv.at[1])
-    prepare(0)
-
-    for ch in range(CHUNKS):
+    def keys_arrive():
+        own_k.wait()
+        own_v.wait()
+        wait(lens.at[0], kv_recv.at[0])
+        wait(raw.at[0], kv_recv.at[1])
+
+    def across(ch):
         spread_wait(ch, 0)
-        r2[ch, 0, z] = pick(owner_x, [r1[ch, 0, i] for i in range(SIDE)])
-        r2[ch, 1, x] = pick(owner_z, [r1[ch, 1, i] for i in range(SIDE)])
+        rows = rows_of(ch)
+        r2[0, z, rows] = pick(owner_x, [r1[0, i, rows] for i in range(SIDE)])
+        r2[1, x, rows] = pick(owner_z, [r1[1, i, rows] for i in range(SIDE)])
         for copy in spread_copies(ch, 1):
             copy.start()
 
-    prepare(1)
-
-    for ch in range(CHUNKS):
+    def gather(ch):
         spread_wait(ch, 1)
-        qf[ch, :, quarter(x, 0)] = pick(owner_z, [r2[ch, 0, i] for i in range(SIDE)])
-        qf[ch, :, quarter(z, 1)] = pick(owner_x, [r2[ch, 1, i] for i in range(SIDE)])
+        rows = rows_of(ch)
+        qf[rows, quarter(x, 0)] = pick(owner_z, [r2[0, i, rows] for i in range(SIDE)])
+        qf[rows, quarter(z, 1)] = pick(owner_x, [r2[1, i, rows] for i in range(SIDE)])
         for copy in spread_copies(ch, 2):
             copy.start()
 
-    diagonal = lax.broadcasted_iota(jnp.int32, (ROWS, 128), 0) == lax.broadcasted_iota(jnp.int32, (ROWS, 128), 1)
+    def diagonal(size):
+        return lax.broadcasted_iota(jnp.int32, (size, 128), 0) == lax.broadcasted_iota(jnp.int32, (size, 128), 1)
 
     def to_row(wide):
-        return jnp.sum(jnp.where(diagonal, wide, 0.0), axis=-2)
-
-    def to_column(row):
-        return jnp.sum(jnp.where(diagonal, row, 0.0), axis=1, keepdims=True)
+        return jnp.sum(jnp.where(diagonal(wide.shape[-2]), wide, 0.0), axis=-2)
+
+    def to_column(row, size):
+        return jnp.sum(jnp.where(diagonal(size), row, 0.0), axis=1, keepdims=True)
 
     def scores(ch, kv):
-        rows = [qf[ch, :, (kv * GROUP + i) * DH : (kv * GROUP + i + 1) * DH] for i in range(GROUP)]
+        rows = [qf[rows_of(ch), (kv * GROUP + i) * DH : (kv * GROUP + i + 1) * DH] for i in range(GROUP)]
         rows = jnp.concatenate(rows, axis=0)
         rows = jnp.concatenate([rows, rows], axis=1)
         return lax.dot_general(rows, kt[kv], AB, preferred_element_type=jnp.float32)
@@ -215,17 +240,17 @@
         partial = jnp.round(both[:, :DH] * (STEPS / largest)).astype(jnp.int32).astype(jnp.int16)
         step = largest * (1.0 / STEPS) / totals
         log_total = highest + jnp.log2(totals)
-        log_rows = to_row(log_total.reshape(GROUP, ROWS, DH))
-        step_rows = to_row(step.reshape(GROUP, ROWS, DH))
+        log_rows = to_row(log_total.reshape(GROUP, SIZES[ch], DH))
+        step_rows = to_row(step.reshape(GROUP, SIZES[ch], DH))
         zi = kv // 2
         for i in range(GROUP):
             xx, core = (kv % 2) * 2 + i // 4, (i % 4) // 2
-            part = partial[i * ROWS : (i + 1) * ROWS]
+            part = partial[i * SIZES[ch] : (i + 1) * SIZES[ch]]
             if i % 2 == 0:
                 place, to, box, stats, count = zi * 2 + core, xx, ca, sa, 4
             else:
                 place, to, box, stats, count = xx * 2 + core, zi, cb, sb, 8
-            box[ch, to, :, place * DH : (place + 1) * DH] = part
+            box[to, rows_of(ch), place * DH : (place + 1) * DH] = part
             stats[ch, to, place : place + 1] = log_rows[i : i + 1]
             stats[ch, to, count + place : count + place + 1] = step_rows[i : i + 1]
 
@@ -235,12 +260,12 @@
         for k in HOPS:
             peer = along_x(k)
             to = device(z, peer, c)
-            act(True, remote(ca.at[ch, peer], ga.at[ch, x], first_send.at[0], first_recv.at[ch, 0], to))
+            act(True, remote(ca.at[peer, rows_of(ch)], ga.at[x, rows_of(ch)], first_send.at[0], first_recv.at[ch, 0], to))
             act(True, remote(sa.at[ch, peer], gsa.at[ch, x], first_send.at[1], first_recv.at[ch, 1], to))
         for zi in range(2):
             zz = 2 * c + zi
             to = device(zz, x, c)
-            act(zz != z, remote(cb.at[ch, zi], gb.at[ch, z], first_send.at[2], first_recv.at[ch, 2], to))
+            act(zz != z, remote(cb.at[zi, rows_of(ch)], gb.at[z, rows_of(ch)], first_send.at[2], first_recv.at[ch, 2], to))
             act(zz != z, remote(sb.at[ch, zi], gsb.at[ch, z], first_send.at[3], first_recv.at[ch, 3], to))
 
     def act_start(condition, copy):
@@ -252,19 +277,26 @@
                 copy.start()
 
     def compute(ch):
-        s = scores(ch, 0)
-        for kv in range(KV_HALF):
-            later = scores(ch, kv + 1) if kv + 1 < KV_HALF else None
+        heads(ch, 0, KV_HALF)
+        push(ch)
+
+    def heads(ch, start, stop):
+        s = scores(ch, start)
+        for kv in range(start, stop):
+            later = scores(ch, kv + 1) if kv + 1 < stop else None
             attend(ch, kv, s)
             s = later
+
+    def push(ch):
         first_copies(ch, act_start)
-        ga[ch, x] = ca[ch, x]
+        rows = rows_of(ch)
+        ga[x, rows] = ca[x, rows]
         gsa[ch, x] = sa[ch, x]
 
         @pl.when(merger)
         def _():
             zi = lax.rem(z, 2)
-            gb[ch, z] = cb[ch, zi]
+            gb[z, rows] = cb[zi, rows]
             gsb[ch, z] = sb[ch, zi]
 
     def weigh(parts):
@@ -282,15 +314,14 @@
             added = functools.reduce(
                 jnp.add,
                 [
-                    to_column(scales[i][head : head + 1]) * got[ch, i, :, cols].astype(jnp.int32).astype(jnp.float32)
+                    to_column(scales[i][head : head + 1], SIZES[ch]) * got[i, rows_of(ch), cols].astype(jnp.int32).astype(jnp.float32)
                     for i in range(SIDE)
                 ],
             )
-            done[ch, head, 0:ROWS] = added
-            done[ch, head, ROWS : ROWS + 8] = jnp.broadcast_to(logs[head : head + 1], (8, 128))
+            done[head, boxed(ch)] = jnp.concatenate([added, jnp.broadcast_to(logs[head : head + 1], (8, 128))], axis=0)
 
     def merge(ch):
-        wait(ga.at[ch, 0 : SIDE - 1], first_recv.at[ch, 0])
+        wait(ga.at[0 : SIDE - 1, rows_of(ch)], first_recv.at[ch, 0])
         wait(gsa.at[ch, 0 : SIDE - 1], first_recv.at[ch, 1])
         merge_side(ch, 4, ga, gsa, da)
         for place in range(4):
@@ -299,17 +330,17 @@
             act_start(
                 jnp.logical_not(here),
                 remote(
-                    da.at[ch, place], ha.at[ch, z], second_send.at[0], second_recv.at[ch, 0], device(zz, x, core)
+                    da.at[place, boxed(ch)], ha.at[z, boxed(ch)], second_send.at[0], second_recv.at[ch, 0], device(zz, x, core)
                 ),
             )
 
             @pl.when(here)
             def _():
-                ha[ch, z] = da[ch, place]
+                ha[z, boxed(ch)] = da[place, boxed(ch)]
 
         @pl.when(merger)
         def _():
-            wait(gb.at[ch, 0 : SIDE - 1], first_recv.at[ch, 2])
+            wait(gb.at[0 : SIDE - 1, rows_of(ch)], first_recv.at[ch, 2])
             wait(gsb.at[ch, 0 : SIDE - 1], first_recv.at[ch, 3])
             merge_side(ch, 8, gb, gsb, db)
             for place in range(8):
@@ -318,55 +349,57 @@
                 act_start(
                     jnp.logical_not(here),
                     remote(
-                        db.at[ch, place], hb.at[ch, x], second_send.at[1], second_recv.at[ch, 1], device(z, xx, core)
+                        db.at[place, boxed(ch)], hb.at[x, boxed(ch)], second_send.at[1], second_recv.at[ch, 1], device(z, xx, core)
                     ),
                 )
 
                 @pl.when(here)
                 def _():
-                    hb[ch, x] = db[ch, place]
+                    hb[x, boxed(ch)] = db[place, boxed(ch)]
 
     def finish(ch):
         for side, got in ((0, ha), (1, hb)):
             @pl.when(merger)
             def _():
-                wait(got.at[ch, 0 : SIDE - 1], second_recv.at[ch, side])
+                wait(got.at[0 : SIDE - 1, boxed(ch)], second_recv.at[ch, side])
 
             @pl.when(jnp.logical_not(merger))
             def _():
-                wait(got.at[ch], second_recv.at[ch, side])
-
-            factors, _ = weigh([got[ch, i, ROWS : ROWS + 1] for i in range(SIDE)])
-            added = functools.reduce(jnp.add, [to_column(factors[i]) * got[ch, i, 0:ROWS] for i in range(SIDE)])
-            out_ref[ch * ROWS : (ch + 1) * ROWS, side * DH : (side + 1) * DH] = added.astype(jnp.bfloat16)
-
-    for ch in range(CHUNKS):
-        spread_wait(ch, 2)
-        compute(ch)
-        if ch > 0:
-            merge(ch - 1)
-    merge(CHUNKS - 1)
-    for ch in range(CHUNKS):
-        finish(ch)
-
-    wait(cand.at[:, 0], core_send)
+                wait(got.at[:, boxed(ch)], second_recv.at[ch, side])
+
+            size, first = SIZES[ch], STARTS[ch] + 8 * ch
+            factors, _ = weigh([got[i, first + size : first + size + 1] for i in range(SIDE)])
+            added = functools.reduce(
+                jnp.add, [to_column(factors[i], size) * got[i, first : first + size] for i in range(SIDE)]
+            )
+            out_ref[rows_of(ch), side * DH : (side + 1) * DH] = added.astype(jnp.bfloat16)
+
+    steps = {
+        "offer": offer, "keys": keys_arrive, "prepare": prepare, "across": across, "gather": gather,
+        "arrive": lambda ch: spread_wait(ch, 2), "heads": heads, "push": push, "compute": compute,
+        "merge": merge, "finish": finish,
+    }
+    for name, *at in ORDER:
+        steps[name](*at)
+
+    wait(cand.at[0], core_send)
     wait(lens.at[0], kv_send.at[0])
     wait(raw.at[0], kv_send.at[1])
     for stage in range(3):
-        wait(r1.at[:, :, 0 : SIDE - 1], q_send.at[stage])
-    wait(ga.at[:, 0 : SIDE - 1], first_send.at[0])
+        wait(r1.at[:, 0 : SIDE - 1], q_send.at[stage])
+    wait(ga.at[0 : SIDE - 1], first_send.at[0])
     wait(gsa.at[:, 0 : SIDE - 1], first_send.at[1])
 
     @pl.when(merger)
     def _():
-        wait(gb.at[:, 0:1], first_send.at[2])
+        wait(gb.at[0:1], first_send.at[2])
         wait(gsb.at[:, 0:1], first_send.at[3])
-        wait(da.at[:, 0:3], second_send.at[0])
-        wait(db.at[:, 0:7], second_send.at[1])
+        wait(da.at[0:3], second_send.at[0])
+        wait(db.at[0:7], second_send.at[1])
 
     @pl.when(jnp.logical_not(merger))
     def _():
-        wait(gb.at[:, 0:2], first_send.at[2])
+        wait(gb.at[0:2], first_send.at[2])
         wait(gsb.at[:, 0:2], first_send.at[3])
         wait(da, second_send.at[0])
 
@@ -382,27 +415,27 @@
         in_specs=[smem, smem, any_space, any_space, any_space],
         out_specs=pl.BlockSpec(memory_space=vmem),
         scratch_shapes=[
-            vmem((CHUNKS, 2, ROWS, HALF), bf16),
-            vmem((CHUNKS, ROWS, HALF), bf16),
-            vmem((CHUNKS, 2, SIDE, ROWS, QUARTER), bf16),
-            vmem((CHUNKS, 2, SIDE, ROWS, QUARTER), bf16),
-            vmem((CHUNKS, ROWS, HALF), bf16),
+            vmem((2, Q, HALF), bf16),
+            vmem((Q, HALF), bf16),
+            vmem((2, SIDE, Q, QUARTER), bf16),
+            vmem((2, SIDE, Q, QUARTER), bf16),
+            vmem((Q, HALF), bf16),
             vmem((2, 2, BLK, KV_HALF * DH), bf16),
             vmem((2, 8, 128), jnp.int32),
             vmem((KV_HALF, 2 * DH, 2 * BLK), bf16),
             vmem((KV_HALF, 2 * BLK, 2 * DH), bf16),
-            vmem((CHUNKS, SIDE, ROWS, 4 * DH), i16),
+            vmem((SIDE, Q, 4 * DH), i16),
             vmem((CHUNKS, SIDE, 8, 128), f32),
-            vmem((CHUNKS, 2, ROWS, 8 * DH), i16),
+            vmem((2, Q, 8 * DH), i16),
             vmem((CHUNKS, 2, 16, 128), f32),
-            vmem((CHUNKS, SIDE, ROWS, 4 * DH), i16),
+            vmem((SIDE, Q, 4 * DH), i16),
             vmem((CHUNKS, SIDE, 8, 128), f32),
-            vmem((CHUNKS, SIDE, ROWS, 8 * DH), i16),
+            vmem((SIDE, Q, 8 * DH), i16),
             vmem((CHUNKS, SIDE, 16, 128), f32),
-            vmem((CHUNKS, 4, ROWS + 8, DH), f32),
-            vmem((CHUNKS, 8, ROWS + 8, DH), f32),
-            vmem((CHUNKS, SIDE, ROWS + 8, DH), f32),
-            vmem((CHUNKS, SIDE, ROWS + 8, DH), f32),
+            vmem((4, Q + 8 * CHUNKS, DH), f32),
+            vmem((8, Q + 8 * CHUNKS, DH), f32),
+            vmem((SIDE, Q + 8 * CHUNKS, DH), f32),
+            vmem((SIDE, Q + 8 * CHUNKS, DH), f32),
             dma, dma((CHUNKS,)),
             dma((2,)), dma((2,)),
             dma((CHUNKS + 2,)),

time: 50.8 us -> 49.6 us (0.976)
  Pallas kernels: 47.9 us -> 46.6 us
    pallas_call x1, Pallas kernels: 47.9 us -> 46.6 us  [on_device(): pl.pallas_call(kernel, out_shape=jax.ShapeDtypeStruct((Q, 2 * DH), bf16),...]
where the time goes in v3:
time: 49.6 us; the launch traced here: 49.4 us
  Pallas kernels  46.6 us (94%)
  local copies, waits for them, and re-layouts  1.47 us (3%)
  between operations  1.31 us (3%)
    pallas_call x1, Pallas kernels, on_device(): pl.pallas_call(kernel, out_shape=jax.ShapeDtypeStruct((Q, 2 * DH), bf16),...  46.6 us
    unnamed x1, local copies, waits for them, and re-layouts  1.47 us

profile of v3, /device:TPU:1, one launch (start us, length us, event | category | flops | bytes accessed | tf_op | source)
XLA Modules:
  0.0 49.4 jit_solution(11203917660296992103)
XLA Ops:
  1.3 46.6 %shard_map.55 = bf16[128,256]{1,0:T(8,128)(2,1)} custom-call(s32[1]{0:T(128)S(6)} %copy.7.lengths_ref, s32[1]{0:T(128)S(6)} %copy.8.owner_ref, bf16[128,8192]{1,0:T(8,128)(2,1)} %queries_ref.1, bf16[1024,1024]{1,0:T(8,128)(2,1)} %keys_ref.1, bf16[1024,1024]{1,0:T(8,128)(2,1)} %values_ref.1), custom_call_target="tpu_custom_call" | custom-call | flops 4294967296 | bytes 6291456 | tf_op jit(solution)/shard_map/pallas_call | solution.py:412
  47.9 1.5 %copy.9 = bf16[128,256]{1,0:T(8,128)(2,1)} copy(bf16[128,256]{1,0:T(8,128)(2,1)} %shard_map.55) | data formatting | bytes 131072

commit v4 on v3

--- a/solution.py
+++ b/solution.py
@@ -29,6 +29,7 @@
 AB = (((1,), (0,)), ((), ()))
 
 
+EARLY = (1,)
 ORDER = (
     *[("offer", ch) for ch in range(CHUNKS)],
     ("keys",),
@@ -95,10 +96,11 @@
         )
 
     barrier = pltpu.get_barrier_semaphore()
-    peers = [sibling]
-    for k in (1, 2, 3):
+    peers = []
+    for k in HOPS:
         for core in range(2):
             peers += [device(z, along_x(k), core), device(along_z(k), x, core)]
+    peers.append(sibling)
     for to in peers:
         pl.semaphore_signal(barrier, inc=1, device_id=to, device_id_type=MESH)
 
@@ -256,18 +258,6 @@
 
     merger = c == z // 2
 
-    def first_copies(ch, act):
-        for k in HOPS:
-            peer = along_x(k)
-            to = device(z, peer, c)
-            act(True, remote(ca.at[peer, rows_of(ch)], ga.at[x, rows_of(ch)], first_send.at[0], first_recv.at[ch, 0], to))
-            act(True, remote(sa.at[ch, peer], gsa.at[ch, x], first_send.at[1], first_recv.at[ch, 1], to))
-        for zi in range(2):
-            zz = 2 * c + zi
-            to = device(zz, x, c)
-            act(zz != z, remote(cb.at[zi, rows_of(ch)], gb.at[z, rows_of(ch)], first_send.at[2], first_recv.at[ch, 2], to))
-            act(zz != z, remote(sb.at[ch, zi], gsb.at[ch, z], first_send.at[3], first_recv.at[ch, 3], to))
-
     def act_start(condition, copy):
         if condition is True:
             copy.start()
@@ -276,28 +266,57 @@
             def _():
                 copy.start()
 
+    def send_or_keep(here, pairs):
+        for src, dst, send, recv, to in pairs:
+            act_start(jnp.logical_not(here), remote(src, dst, send, recv, to))
+
+        @pl.when(here)
+        def _():
+            for src, dst, *_ in pairs:
+                dst[...] = src[...]
+
+    def push_x(ch, xx):
+        to, rows = device(z, xx, c), rows_of(ch)
+        send_or_keep(
+            xx == x,
+            [
+                (ca.at[xx, rows], ga.at[x, rows], first_send.at[0], first_recv.at[ch, 0], to),
+                (sa.at[ch, xx], gsa.at[ch, x], first_send.at[1], first_recv.at[ch, 1], to),
+            ],
+        )
+
+    def push_z(ch, zi):
+        to, rows = device(2 * c + zi, x, c), rows_of(ch)
+        send_or_keep(
+            2 * c + zi == z,
+            [
+                (cb.at[zi, rows], gb.at[z, rows], first_send.at[2], first_recv.at[ch, 2], to),
+                (sb.at[ch, zi], gsb.at[ch, z], first_send.at[3], first_recv.at[ch, 3], to),
+            ],
+        )
+
     def compute(ch):
-        heads(ch, 0, KV_HALF)
-        push(ch)
-
-    def heads(ch, start, stop):
-        s = scores(ch, start)
-        for kv in range(start, stop):
-            later = scores(ch, kv + 1) if kv + 1 < stop else None
+        s = scores(ch, 0)
+        for kv in range(KV_HALF):
+            later = scores(ch, kv + 1) if kv + 1 < KV_HALF else None
             attend(ch, kv, s)
             s = later
-
-    def push(ch):
-        first_copies(ch, act_start)
-        rows = rows_of(ch)
-        ga[x, rows] = ca[x, rows]
-        gsa[ch, x] = sa[ch, x]
-
-        @pl.when(merger)
-        def _():
-            zi = lax.rem(z, 2)
-            gb[z, rows] = cb[zi, rows]
-            gsb[ch, z] = sb[ch, zi]
+            if kv in EARLY:
+                push(ch, kv)
+        for kv in range(KV_HALF):
+            if kv not in EARLY:
+                push(ch, kv)
+
+    def push(ch, kv):
+        if kv == 1:
+            push_z(ch, 0)
+        if kv == 2:
+            push_x(ch, 0)
+            push_x(ch, 1)
+        if kv == 3:
+            push_x(ch, 2)
+            push_x(ch, 3)
+            push_z(ch, 1)
 
     def weigh(parts):
         top = functools.reduce(jnp.maximum, parts)
@@ -376,7 +395,7 @@
 
     steps = {
         "offer": offer, "keys": keys_arrive, "prepare": prepare, "across": across, "gather": gather,
-        "arrive": lambda ch: spread_wait(ch, 2), "heads": heads, "push": push, "compute": compute,
+        "arrive": lambda ch: spread_wait(ch, 2), "compute": compute,
         "merge": merge, "finish": finish,
     }
     for name, *at in ORDER:

time: 49.6 us -> 49.2 us (level)
  no operation moved by 1% of the time
where the time goes in v4:
time: 49.2 us; the launch traced here: 49 us
  Pallas kernels  46.2 us (94%)
  local copies, waits for them, and re-layouts  1.47 us (3%)
  between operations  1.31 us (3%)
    pallas_call x1, Pallas kernels, on_device(): pl.pallas_call(kernel, out_shape=jax.ShapeDtypeStruct((Q, 2 * DH), bf16),...  46.2 us
    unnamed x1, local copies, waits for them, and re-layouts  1.47 us

profile of v4, /device:TPU:1, one launch (start us, length us, event | category | flops | bytes accessed | tf_op | source)
XLA Modules:
  0.0 49.0 jit_solution(17192309249355729946)
XLA Ops:
  1.3 46.2 %shard_map.55 = bf16[128,256]{1,0:T(8,128)(2,1)} custom-call(s32[1]{0:T(128)S(6)} %copy.7.lengths_ref, s32[1]{0:T(128)S(6)} %copy.8.owner_ref, bf16[128,8192]{1,0:T(8,128)(2,1)} %queries_ref.1, bf16[1024,1024]{1,0:T(8,128)(2,1)} %keys_ref.1, bf16[1024,1024]{1,0:T(8,128)(2,1)} %values_ref.1), custom_call_target="tpu_custom_call" | custom-call | flops 4294967296 | bytes 6291456 | tf_op jit(solution)/shard_map/pallas_call | solution.py:431
  47.5 1.5 %copy.9 = bf16[128,256]{1,0:T(8,128)(2,1)} copy(bf16[128,256]{1,0:T(8,128)(2,1)} %shard_map.55) | data formatting | bytes 131072

commit v5 on v4

--- a/solution.py
+++ b/solution.py
@@ -29,7 +29,7 @@
 AB = (((1,), (0,)), ((), ()))
 
 
-EARLY = (1,)
+EARLY = ((), (), (1, 2))
 ORDER = (
     *[("offer", ch) for ch in range(CHUNKS)],
     ("keys",),
@@ -301,10 +301,10 @@
             later = scores(ch, kv + 1) if kv + 1 < KV_HALF else None
             attend(ch, kv, s)
             s = later
-            if kv in EARLY:
+            if kv in EARLY[ch]:
                 push(ch, kv)
         for kv in range(KV_HALF):
-            if kv not in EARLY:
+            if kv not in EARLY[ch]:
                 push(ch, kv)
 
     def push(ch, kv):

time: 49.2 us -> 49.9 us (1.014)
  Pallas kernels: 46.2 us -> 46.9 us
    pallas_call x1, Pallas kernels: 46.2 us -> 46.9 us  [on_device(): pl.pallas_call(kernel, out_shape=jax.ShapeDtypeStruct((Q, 2 * DH), bf16),...]
where the time goes in v5:
time: 49.9 us; the launch traced here: 49.7 us
  Pallas kernels  46.9 us (94%)
  local copies, waits for them, and re-layouts  1.47 us (3%)
  between operations  1.31 us (3%)
    pallas_call x1, Pallas kernels, on_device(): pl.pallas_call(kernel, out_shape=jax.ShapeDtypeStruct((Q, 2 * DH), bf16),...  46.9 us
    unnamed x1, local copies, waits for them, and re-layouts  1.47 us

profile of v5, /device:TPU:1, one launch (start us, length us, event | category | flops | bytes accessed | tf_op | source)
XLA Modules:
  0.0 49.7 jit_solution(2636178648375245892)
XLA Ops:
  1.3 46.9 %shard_map.55 = bf16[128,256]{1,0:T(8,128)(2,1)} custom-call(s32[1]{0:T(128)S(6)} %copy.7.lengths_ref, s32[1]{0:T(128)S(6)} %copy.8.owner_ref, bf16[128,8192]{1,0:T(8,128)(2,1)} %queries_ref.1, bf16[1024,1024]{1,0:T(8,128)(2,1)} %keys_ref.1, bf16[1024,1024]{1,0:T(8,128)(2,1)} %values_ref.1), custom_call_target="tpu_custom_call" | custom-call | flops 4294967296 | bytes 6291456 | tf_op jit(solution)/shard_map/pallas_call | solution.py:431
  48.3 1.5 %copy.9 = bf16[128,256]{1,0:T(8,128)(2,1)} copy(bf16[128,256]{1,0:T(8,128)(2,1)} %shard_map.55) | data formatting | bytes 131072
